TPU v7x, 32 devices: a whole 2x2x4 slice. The times are simulated.
32 devices in a mesh: row: 8 (over y, x, core), col: 4 (over z).
Axes of the slice: x: 2, y: 2, z: 4, core: 2. Of those that a mesh axis runs over, the one named last changes fastest.
Arguments:
- picture_encoder_output: bfloat16 [6144, 1152], P(('row', 'col')), may hold values from -0.59765625 to 0.59765625
- caption_encoder_output: bfloat16 [6144, 1152], P(('row', 'col')), may hold values from -0.59765625 to 0.59765625
- softness_factor_exponent: float32 [], replicated, may hold values from 2.7 to 3.7
- logit_offset_term: float32 [], replicated, may hold values from -5 to -2
Outputs:
- image_grad: float32 [6144, 1152], P(('row', 'col'))
- text_grad: float32 [6144, 1152], P(('row', 'col'))
All inputs are finite; a program needn't handle non-finite values.
Results may differ from a plain program's by a relative error of at most 0.008.
Values may be sent and summed in bfloat16 or wider, within the bound.
No kernel may reach another device: no remote copies, remote signals or barrier semaphores. Data moves between devices by JAX's collectives and lax.ppermute only.
A program may use at most 64 MiB of HBM per device.

v0:
```python
import functools

import jax
import jax.numpy as jnp
from jax import lax
from jax.experimental import pallas as pl
from jax.experimental.pallas import tpu as pltpu
from jax.sharding import PartitionSpec as P

eps_norm = 1e-06
VMEM = pl.BlockSpec(memory_space=pltpu.VMEM)
SMEM = pl.BlockSpec(memory_space=pltpu.SMEM)
HBM = pl.BlockSpec(memory_space=pltpu.HBM)
LIMIT = 24 * 2**20
PIECES = 4


def along(value, axis, target):
    count = lax.axis_size(axis)
    pairs = [(source, target(source) % count) for source in range(count)]
    return lax.ppermute(value, axis, pairs)


def inverse_norm(values):
    return lax.rsqrt(jnp.sum(values * values, axis=-1, keepdims=True) + eps_norm)


def unit_half(raw):
    values = raw.astype(jnp.float32)
    return (values * inverse_norm(values)).astype(jnp.bfloat16)


def weigh(own, other, temperature, offset):
    scores = lax.dot_general(
        own, other, (((1,), (1,)), ((), ())), preferred_element_type=jnp.float32
    )
    return jax.nn.sigmoid(temperature * scores + offset)


def visit(own, other, temperature, offset):
    weights = temperature * weigh(own, other, temperature, offset)
    return jnp.dot(weights.astype(jnp.bfloat16), other, preferred_element_type=jnp.float32)


def unit_back(raw, direction):
    values = raw.astype(jnp.float32)
    inverse = inverse_norm(values)
    unit = values * inverse
    share = jnp.sum(unit * direction, axis=-1, keepdims=True)
    return inverse * (direction - unit * share)


def pieces(rows):
    if rows % (16 * PIECES):
        return [(0, rows)]
    return [(n * rows // PIECES, rows // PIECES) for n in range(PIECES)]


def call(kernel, out_shape, in_specs, out_specs, **more):
    return pl.pallas_call(
        kernel,
        out_shape=out_shape,
        in_specs=in_specs,
        out_specs=out_specs,
        compiler_params=pltpu.CompilerParams(vmem_limit_bytes=LIMIT),
        cost_estimate=pl.CostEstimate(flops=1000, bytes_accessed=1000, transcendentals=0),
        **more,
    )


def norm_kernel(odd_ref, img_ref, txt_ref, raw_ref, half_ref, img_half, far_ref, near_ref, sems):
    parts = pieces(img_ref.shape[0])
    copies = []
    for side, source in ((0, img_ref), (1, txt_ref)):
        for n, (start, size) in enumerate(parts):
            at = pl.ds(start, size)
            copies.append(
                pltpu.make_async_copy(source.at[at], raw_ref.at[side, at], sems.at[side, n])
            )
    for copy in copies:
        copy.start()
    for side in (0, 1):
        for n, (start, size) in enumerate(parts):
            copies[side * len(parts) + n].wait()
            at = pl.ds(start, size)
            half_ref[side, at] = unit_half(raw_ref[side, at])
            if side == 0:
                img_half[at] = half_ref[side, at]
    far_ref[...] = half_ref[odd_ref[0]]
    near_ref[...] = half_ref[1 - odd_ref[0]]


def norm(odd, img, txt):
    rows, width = img.shape
    one = jax.ShapeDtypeStruct((rows, width), jnp.bfloat16)
    both = jax.ShapeDtypeStruct((2, rows, width), jnp.bfloat16)
    return call(
        norm_kernel,
        (both, both, one, one, one),
        [SMEM, HBM, HBM],
        (VMEM,) * 5,
        scratch_shapes=[pltpu.SemaphoreType.DMA((2, len(pieces(rows))))],
        name="norm",
    )(odd, img, txt)


def own_kernel(scale_ref, half_ref, dir_ref):
    temperature, offset = scale_ref[0], scale_ref[1]
    img, txt = half_ref[0], half_ref[1]
    rows = img.shape[0]
    row = lax.broadcasted_iota(jnp.int32, (rows, rows), 0)
    column = lax.broadcasted_iota(jnp.int32, (rows, rows), 1)
    match = jnp.where(row == column, 1.0, 0.0)
    weights = (temperature * (weigh(img, txt, temperature, offset) - match)).astype(jnp.bfloat16)
    dir_ref[0] = jnp.dot(weights, txt, preferred_element_type=jnp.float32)
    weights = (temperature * (weigh(txt, img, temperature, offset) - match)).astype(jnp.bfloat16)
    dir_ref[1] = jnp.dot(weights, img, preferred_element_type=jnp.float32)


def own_visit(scale, half):
    return call(
        own_kernel,
        jax.ShapeDtypeStruct(half.shape, jnp.float32),
        [SMEM, VMEM],
        VMEM,
        name="own",
    )(scale, half)


def visit_all(kinds, blocks, scale_ref, odd_ref, half_ref, acc_ref):
    for (side, raw), block in zip(kinds, blocks):
        other = unit_half(block[...]) if raw else block[...]
        at = side if side < 2 else odd_ref[0] if side == 2 else 1 - odd_ref[0]
        acc_ref[at] += visit(half_ref[at], other, scale_ref[0], scale_ref[1])


def more_kernel(kinds, scale_ref, odd_ref, half_ref, dir_ref, *rest):
    blocks, out_ref = rest[:-1], rest[-1]
    out_ref[...] = dir_ref[...]
    visit_all(kinds, blocks, scale_ref, odd_ref, half_ref, out_ref)


def finish(raw_ref, acc_ref, grad_ref, held_ref, sems):
    copies = []
    for n, (start, size) in enumerate(pieces(held_ref.shape[0])):
        at = pl.ds(start, size)
        held_ref[at] = unit_back(raw_ref[at], acc_ref[at])
        copies.append(pltpu.make_async_copy(held_ref.at[at], grad_ref.at[at], sems.at[n]))
        copies[-1].start()
    return copies


def image_kernel(kinds, scale_ref, odd_ref, half_ref, dir_ref, raw_ref, *rest):
    blocks, (out_ref, grad_ref, held_ref, sems) = rest[:-4], rest[-4:]
    out_ref[...] = dir_ref[...]
    visit_all(kinds, blocks, scale_ref, odd_ref, half_ref, out_ref)
    for copy in finish(raw_ref.at[0], out_ref.at[0], grad_ref, held_ref, sems):
        copy.wait()


def text_kernel(kinds, scale_ref, odd_ref, half_ref, dir_ref, raw_ref, *rest):
    blocks, (grad_ref, acc_ref, held_ref, sems) = rest[:-4], rest[-4:]
    acc_ref[1] = dir_ref[1]
    visit_all(kinds, blocks, scale_ref, odd_ref, half_ref, acc_ref)
    for copy in finish(raw_ref.at[1], acc_ref.at[1], grad_ref, held_ref, sems):
        copy.wait()


def visits(kernel, scale, odd, half, direction, entries, raw=None):
    kinds, blocks = zip(*entries) if entries else ((), ())
    rows, width = half.shape[1:]
    same = jax.ShapeDtypeStruct(direction.shape, direction.dtype)
    grad = jax.ShapeDtypeStruct((rows, width), jnp.float32)
    operands = [scale, odd, half, direction] + ([] if raw is None else [raw])
    held = [pltpu.VMEM(grad.shape, grad.dtype), pltpu.SemaphoreType.DMA((len(pieces(rows)),))]
    if kernel is more_kernel:
        out_shape, out_specs, held, aliases = same, VMEM, [], {3: 0}
    elif kernel is image_kernel:
        out_shape, out_specs, aliases = (same, grad), (VMEM, HBM), {3: 0}
    else:
        out_shape, out_specs, aliases = grad, HBM, {}
        held = [pltpu.VMEM(same.shape, same.dtype)] + held
    return call(
        functools.partial(kernel, kinds),
        out_shape,
        [SMEM, SMEM] + [VMEM] * (len(operands) - 2 + len(blocks)),
        out_specs,
        input_output_aliases=aliases,
        scratch_shapes=held,
        name=kernel.__name__,
    )(*operands, *blocks)


def on_device(
    picture_encoder_output, caption_encoder_output, softness_factor_exponent, logit_offset_term
):
    img, txt = picture_encoder_output, caption_encoder_output
    row_extent = min(8, lax.axis_size("row") // 2)
    column_extent = min(4, lax.axis_size("col") // 2)
    odd = (lax.axis_index("row") & 1).astype(jnp.int32).reshape(1)
    scale = jnp.stack([jnp.exp(softness_factor_exponent), logit_offset_term])
    paired = row_extent % 2 == 0 and lax.axis_size("row") % 2 == 0
    swap = lambda s: s ^ 1
    held = [pltpu.with_memory_space_constraint(a, pltpu.HBM) for a in (img, txt)]
    raw, half, img_half, far, near = norm(odd, *held)

    def tied(entries, *others):
        blocks, others = lax.optimization_barrier(([block for _, block in entries], others))
        return [(kind, block) for (kind, _), block in zip(entries, blocks)], *others

    text_cols, image_cols, text_rows, image_rows, swapped, last = [], [], [], [], [], []
    for k in range(1, column_extent):
        text_cols.append(((0, True), along(txt, "col", lambda s: s + k)))
    direction = own_visit(scale, half)
    tied_cols, col_half, direction = tied(text_cols, img_half, direction)
    for k in range(1, column_extent):
        image_cols.append(((1, False), along(col_half, "col", lambda s: s - k)))
    direction = visits(more_kernel, scale, odd, half, direction, tied_cols)
    if paired:
        for d in range(2, row_extent, 2):
            text_rows.append(((0, True), along(txt, "row", lambda s: s + d)))
            image_rows.append(((1, False), along(img_half, "row", lambda s: s - d)))
        reach = row_extent - 1
        far = [((2, False), along(far, "row", lambda s: s + reach if s % 2 else s - reach))]
        direction = visits(more_kernel, scale, odd, half, direction, text_rows)
        tied_rows, near, direction = tied(text_rows, near, direction)
        swapped.append(((3, False), along(near, "row", swap)))
        for kind, block in tied_rows:
            swapped.append((kind, along(block, "row", swap)))
        count = len(image_rows)
        rest, direction = tied(image_rows + image_cols + far, direction)
        for kind, block in rest[:count]:
            last.append((kind, along(block, "row", swap)))
        middle = rest + swapped
    else:
        middle = image_cols
        for k in range(1, row_extent):
            middle.append(((0, True), along(txt, "row", lambda s: s + k)))
            middle.append(((1, True), along(img, "row", lambda s: s - k)))

    direction, image_grad = visits(image_kernel, scale, odd, half, direction, middle, raw)
    return image_grad, visits(text_kernel, scale, odd, half, direction, last, raw)


def solution(mesh):
    return jax.shard_map(
        on_device,
        mesh=mesh,
        in_specs=(P(("row", "col"), None), P(("row", "col"), None), P(), P()),
        out_specs=(P(("row", "col"), None), P(("row", "col"), None)),
        check_vma=False,
    )
```

profile of v0, /device:TPU:19, one launch (start us, length us, event | category | flops | bytes accessed | tf_op | source)
XLA Modules:
  0.0 37.1 jit_solution(1797704466311453577)
XLA Ops:
  0.6 1.3 %collective-permute-start.1 = (bf16[192,1152]{1,0:T(8,128)(2,1)}, bf16[192,1152]{1,0:T(8,128)(2,1)S(1)}, u32[]{:S(2)}, u32[]{:S(2)}) collective-permute-start(bf16[192,1152]{1,0:T(8,128)(2,1)} %txt_ref.1), channel_id=1, source_target_pairs={{0,1},{1,2},{2,3},{3,0},{4,5},{5,6},{6,7},{7,4},{8,9},{9,10},{10,1... | collective-permute-start | bytes 1327112 | tf_op jit(solution)/shard_map/ppermute | solution.py:21
  2.0 1.2 %collective-permute-start.4 = (bf16[192,1152]{1,0:T(8,128)(2,1)}, bf16[192,1152]{1,0:T(8,128)(2,1)S(1)}, u32[]{:S(2)}, u32[]{:S(2)}) collective-permute-start(bf16[192,1152]{1,0:T(8,128)(2,1)} %txt_ref.1), channel_id=1, source_target_pairs={{0,8},{4,12},{8,16},{12,20},{16,24},{20,28},{24,0},{28,4},{1,9},{5... | collective-permute-start | bytes 1327112 | tf_op jit(solution)/shard_map/ppermute | solution.py:21
  3.2 2.7 %norm.1 = (bf16[2,192,1152]{2,1,0:T(8,128)(2,1)S(1)}, bf16[2,192,1152]{2,1,0:T(8,128)(2,1)S(1)}, bf16[192,1152]{1,0:T(8,128)(2,1)}, bf16[192,1152]{1,0:T(8,128)(2,1)}, bf16[192,1152]{1,0:T(8,128)(2,1)S(1)}) custom-call(s32[1]{0:T(128)} %bitcast.2.odd_ref, bf16[192,1152]{1,0:T(8,128)(2,1)} %img_ref.1, bf16[192,1152]{1,0:T(8,128)(2,1)} %txt_ref.1), custom_call_target="tpu_custom_call" | custom-call | flops 1000 | bytes 1000 | tf_op jit(solution)/shard_map/norm/pallas_call | solution.py:97
  6.0 0.8 %copy-done = bf16[192,1152]{1,0:T(8,128)(2,1)} copy-done((bf16[192,1152]{1,0:T(8,128)(2,1)}, bf16[192,1152]{1,0:T(8,128)(2,1)S(1)}, u32[]{:S(2)}) %copy-start) | copy-done | bytes 442392
  6.7 0.3 collective-permute-start
  7.0 2.6 %collective-permute-start.3 = (bf16[192,1152]{1,0:T(8,128)(2,1)}, bf16[192,1152]{1,0:T(8,128)(2,1)S(1)}, u32[]{:S(2)}, u32[]{:S(2)}) collective-permute-start(bf16[192,1152]{1,0:T(8,128)(2,1)} %get-tuple-element.22), channel_id=1, source_target_pairs={{0,20},{4,16},{8,28},{12,24},{16,4},{20,0},{24,12},{28,8},{1,21},{... | collective-permute-start | bytes 1327112 | tf_op jit(solution)/shard_map/ppermute | solution.py:21
  10.9 0.1 pad_maximum_fusion.scale_ref
  11.0 1.9 %own.1.dir_ref = f32[2,192,1152]{2,1,0:T(8,128)S(1)} custom-call(f32[2]{0:T(128)S(1)} %pad_maximum_fusion.scale_ref, bf16[2,192,1152]{2,1,0:T(8,128)(2,1)S(1)} %get-tuple-element.19.half_ref), custom_call_target="tpu_custom_call" | custom-call | flops 1000 | bytes 1000 | tf_op jit(solution)/shard_map/own/pallas_call | solution.py:121
  12.9 0.0 collective-permute-done.1.rest_0_
  12.9 0.2 collective-permute-start.2
  13.1 1.5 %more_kernel.2.dir_ref = f32[2,192,1152]{2,1,0:T(8,128)S(1)} custom-call(f32[2]{0:T(128)S(1)} %pad_maximum_fusion.scale_ref, s32[1]{0:T(128)} %bitcast.2.odd_ref, bf16[2,192,1152]{2,1,0:T(8,128)(2,1)S(1)} %get-tuple-element.19.half_ref, f32[2,192,1152]{2,1,0:T(8,128)S(1)} %own.1.dir_ref, ...), custom_call_target="tpu_custom_call", output_to_operand_aliasing={{}: (3, {})} | custom-call | flops 1000 | bytes 1000 | tf_op jit(solution)/shard_map/more_kernel/pallas_call | solution.py:183
  14.7 0.0 collective-permute-done.4.rest_0_
  14.7 1.6 %more_kernel.3.dir_ref = f32[2,192,1152]{2,1,0:T(8,128)S(1)} custom-call(f32[2]{0:T(128)S(1)} %pad_maximum_fusion.scale_ref, s32[1]{0:T(128)} %bitcast.2.odd_ref, bf16[2,192,1152]{2,1,0:T(8,128)(2,1)S(1)} %get-tuple-element.19.half_ref, f32[2,192,1152]{2,1,0:T(8,128)S(1)} %more_kernel.2.dir_ref, ...), custom_call_target="tpu_custom_call", output_to_operand_aliasing={{}: (3, {})} | custom-call | flops 1000 | bytes 1000 | tf_op jit(solution)/shard_map/more_kernel/pallas_call | solution.py:183
  16.3 1.6 %collective-permute-start.5 = (bf16[192,1152]{1,0:T(8,128)(2,1)S(1)}, bf16[192,1152]{1,0:T(8,128)(2,1)S(1)}, u32[]{:S(2)}, u32[]{:S(2)}) collective-permute-start(bf16[192,1152]{1,0:T(8,128)(2,1)S(1)} %copy-done.1), channel_id=1, source_target_pairs={{0,4},{4,0},{8,12},{12,8},{16,20},{20,16},{24,28},{28,24},{1,5},{5... | collective-permute-start | bytes 1327112 | tf_op jit(solution)/shard_map/ppermute | solution.py:21
  17.9 0.1 collective-permute-start.6
  17.9 5.4 %collective-permute-done.rest_0_ = bf16[192,1152]{1,0:T(8,128)(2,1)S(1)} collective-permute-done((bf16[192,1152]{1,0:T(8,128)(2,1)}, bf16[192,1152]{1,0:T(8,128)(2,1)S(1)}, u32[]{:S(2)}, u32[]{:S(2)}) %collective-permute-start) | collective-permute-done | bytes 442400 | tf_op jit(solution)/shard_map/ppermute | solution.py:21
  23.4 6.8 %collective-permute-done.3.rest_2_ = bf16[192,1152]{1,0:T(8,128)(2,1)S(1)} collective-permute-done((bf16[192,1152]{1,0:T(8,128)(2,1)}, bf16[192,1152]{1,0:T(8,128)(2,1)S(1)}, u32[]{:S(2)}, u32[]{:S(2)}) %collective-permute-start.3) | collective-permute-done | bytes 442400 | tf_op jit(solution)/shard_map/ppermute | solution.py:21
  30.2 0.0 collective-permute-done.2.rest_1_
  30.2 0.4 %collective-permute-start.7 = (bf16[192,1152]{1,0:T(8,128)(2,1)S(1)}, bf16[192,1152]{1,0:T(8,128)(2,1)S(1)}, u32[]{:S(2)}, u32[]{:S(2)}) collective-permute-start(bf16[192,1152]{1,0:T(8,128)(2,1)S(1)} %collective-permute-done.rest_0_), channel_id=1, source_target_pairs={{0,4},{4,0},{8,12},{12,8},{16,20},{20,16},{24,28},{28,24},{1,5},{5... | collective-permute-start | bytes 1327112 | tf_op jit(solution)/shard_map/ppermute | solution.py:21
  30.6 0.0 collective-permute-done.5.rest_3_
  30.6 0.0 collective-permute-done.6.rest_4_
  30.6 4.1 %image_kernel.1 = (f32[2,192,1152]{2,1,0:T(8,128)S(1)}, f32[192,1152]{1,0:T(8,128)}) custom-call(f32[2]{0:T(128)S(1)} %pad_maximum_fusion.scale_ref, s32[1]{0:T(128)} %bitcast.2.odd_ref, bf16[2,192,1152]{2,1,0:T(8,128)(2,1)S(1)} %get-tuple-element.19.half_ref, f32[2,192,1152]{2,1,0:T(8,128)S(1)} %more_kernel.3.dir_ref, ...), custom_call_target="tpu_custom_call", output_to_operand_aliasing={{0}: (3, {})} | custom-call | flops 1000 | bytes 1000 | tf_op jit(solution)/shard_map/image_kernel/pallas_call | solution.py:183
  34.7 0.0 collective-permute-done.7.rest_0_
  34.7 2.4 %text_kernel.1 = f32[192,1152]{1,0:T(8,128)} custom-call(f32[2]{0:T(128)S(1)} %pad_maximum_fusion.scale_ref, s32[1]{0:T(128)} %bitcast.2.odd_ref, bf16[2,192,1152]{2,1,0:T(8,128)(2,1)S(1)} %get-tuple-element.19.half_ref, f32[2,192,1152]{2,1,0:T(8,128)S(1)} %get-tuple-element.35.dir_ref, bf16[2,192,1152]{2,1,0:T(8,128)(2,1)S(1)} %get-tuple-element.28.raw_ref, ...), custom_call_target="tpu_custom_call" | custom-call | flops 1000 | bytes 1000 | tf_op jit(solution)/shard_map/text_kernel/pallas_call | solution.py:183
  (3 shorter events, 0.0 us)
Async XLA Ops:
  0.6 12.3 %collective-permute-start.1 = (bf16[192,1152]{1,0:T(8,128)(2,1)}, bf16[192,1152]{1,0:T(8,128)(2,1)S(1)}, u32[]{:S(2)}, u32[]{:S(2)}) collective-permute-start(bf16[192,1152]{1,0:T(8,128)(2,1)} %txt_ref.1), channel_id=1, source_target_pairs={{0,1},{1,2},{2,3},{3,0},{4,5},{5,6},{6,7},{7,4},{8,9},{9,10},{10,1... | collective-permute-start | bytes 1327112 | tf_op jit(solution)/shard_map/ppermute | solution.py:21
  2.0 12.7 %collective-permute-start.4 = (bf16[192,1152]{1,0:T(8,128)(2,1)}, bf16[192,1152]{1,0:T(8,128)(2,1)S(1)}, u32[]{:S(2)}, u32[]{:S(2)}) collective-permute-start(bf16[192,1152]{1,0:T(8,128)(2,1)} %txt_ref.1), channel_id=1, source_target_pairs={{0,8},{4,12},{8,16},{12,20},{16,24},{20,28},{24,0},{28,4},{1,9},{5... | collective-permute-start | bytes 1327112 | tf_op jit(solution)/shard_map/ppermute | solution.py:21
  5.9 0.8 %copy-start = (bf16[192,1152]{1,0:T(8,128)(2,1)}, bf16[192,1152]{1,0:T(8,128)(2,1)S(1)}, u32[]{:S(2)}) copy-start(bf16[192,1152]{1,0:T(8,128)(2,1)S(1)} %get-tuple-element.32) | copy-start | bytes 1327108
  6.7 16.7 %collective-permute-start = (bf16[192,1152]{1,0:T(8,128)(2,1)}, bf16[192,1152]{1,0:T(8,128)(2,1)S(1)}, u32[]{:S(2)}, u32[]{:S(2)}) collective-permute-start(bf16[192,1152]{1,0:T(8,128)(2,1)} %get-tuple-element.21), channel_id=1, source_target_pairs={{0,24},{4,28},{8,0},{12,4},{16,8},{20,12},{24,16},{28,20},{1,25},{... | collective-permute-start | bytes 1327112 | tf_op jit(solution)/shard_map/ppermute | solution.py:21
  7.0 23.2 %collective-permute-start.3 = (bf16[192,1152]{1,0:T(8,128)(2,1)}, bf16[192,1152]{1,0:T(8,128)(2,1)S(1)}, u32[]{:S(2)}, u32[]{:S(2)}) collective-permute-start(bf16[192,1152]{1,0:T(8,128)(2,1)} %get-tuple-element.22), channel_id=1, source_target_pairs={{0,20},{4,16},{8,28},{12,24},{16,4},{20,0},{24,12},{28,8},{1,21},{... | collective-permute-start | bytes 1327112 | tf_op jit(solution)/shard_map/ppermute | solution.py:21
  12.9 17.3 %collective-permute-start.2 = (bf16[192,1152]{1,0:T(8,128)(2,1)}, bf16[192,1152]{1,0:T(8,128)(2,1)S(1)}, u32[]{:S(2)}, u32[]{:S(2)}) collective-permute-start(bf16[192,1152]{1,0:T(8,128)(2,1)} %get-tuple-element.21), channel_id=1, source_target_pairs={{0,3},{1,0},{2,1},{3,2},{4,7},{5,4},{6,5},{7,6},{8,11},{9,8},{10,9... | collective-permute-start | bytes 1327112 | tf_op jit(solution)/shard_map/ppermute | solution.py:21
  14.7 1.6 %copy-start.1 = (bf16[192,1152]{1,0:T(8,128)(2,1)S(1)}, bf16[192,1152]{1,0:T(8,128)(2,1)}, u32[]{:S(2)}) copy-start(bf16[192,1152]{1,0:T(8,128)(2,1)} %copy-done) | copy-start | bytes 1327108
  16.3 14.3 %collective-permute-start.5 = (bf16[192,1152]{1,0:T(8,128)(2,1)S(1)}, bf16[192,1152]{1,0:T(8,128)(2,1)S(1)}, u32[]{:S(2)}, u32[]{:S(2)}) collective-permute-start(bf16[192,1152]{1,0:T(8,128)(2,1)S(1)} %copy-done.1), channel_id=1, source_target_pairs={{0,4},{4,0},{8,12},{12,8},{16,20},{20,16},{24,28},{28,24},{1,5},{5... | collective-permute-start | bytes 1327112 | tf_op jit(solution)/shard_map/ppermute | solution.py:21
  17.9 12.7 %collective-permute-start.6 = (bf16[192,1152]{1,0:T(8,128)(2,1)S(1)}, bf16[192,1152]{1,0:T(8,128)(2,1)S(1)}, u32[]{:S(2)}, u32[]{:S(2)}) collective-permute-start(bf16[192,1152]{1,0:T(8,128)(2,1)S(1)} %collective-permute-done.4.rest_0_), channel_id=1, source_target_pairs={{0,4},{4,0},{8,12},{12,8},{16,20},{20,16},{24,28},{28,24},{1,5},{5... | collective-permute-start | bytes 1327112 | tf_op jit(solution)/shard_map/ppermute | solution.py:21
  30.2 4.5 %collective-permute-start.7 = (bf16[192,1152]{1,0:T(8,128)(2,1)S(1)}, bf16[192,1152]{1,0:T(8,128)(2,1)S(1)}, u32[]{:S(2)}, u32[]{:S(2)}) collective-permute-start(bf16[192,1152]{1,0:T(8,128)(2,1)S(1)} %collective-permute-done.rest_0_), channel_id=1, source_target_pairs={{0,4},{4,0},{8,12},{12,8},{16,20},{20,16},{24,28},{28,24},{1,5},{5... | collective-permute-start | bytes 1327112 | tf_op jit(solution)/shard_map/ppermute | solution.py:21
where the time goes:
time: 37.2 us; the launch traced here: 37.1 us
  Pallas kernels  14.2 us (38%)
  waiting for transfers between devices  12.2 us (33%)
  starting transfers between devices  7.76 us (21%)
  between operations  2.06 us (6%)
  local copies, waits for them, and re-layouts  0.76 us (2%)
    ppermute x8, waiting for transfers between devices, along(): return lax.ppermute(value, axis, pairs)  12.2 us
    pallas_call x4, Pallas kernels, visits(): call(functools.partial(kernel, kinds), out_shape, [SMEM, SMEM] + [VMEM] *...  9.58 us
    ppermute x8, starting transfers between devices, along(): return lax.ppermute(value, axis, pairs)  7.76 us
    pallas_call x1, Pallas kernels, norm(): call(norm_kernel, (both, both, one, one, one), [SMEM, HBM, HBM], (VMEM,)...  2.75 us
    pallas_call x1, Pallas kernels, own_visit(): call(own_kernel, jax.ShapeDtypeStruct(half.shape, jnp.float32), [SMEM, VM...  1.86 us
    unnamed x4, local copies, waits for them, and re-layouts  0.76 us
  transfers between devices with their start and end apart: 8, of which 2 were waited for; matrix products, arithmetic and copies ran while one was open for 0% of the time, Pallas kernels for 32%

commit v1 on v0

v1 whole, which is shorter than its diff:
```python
import functools

import jax
import jax.numpy as jnp
from jax import lax
from jax.experimental import pallas as pl
from jax.experimental.pallas import tpu as pltpu
from jax.sharding import PartitionSpec as P

eps_norm = 1e-06
VMEM = pl.BlockSpec(memory_space=pltpu.VMEM)
SMEM = pl.BlockSpec(memory_space=pltpu.SMEM)
HBM = pl.BlockSpec(memory_space=pltpu.HBM)
LIMIT = 24 * 2**20
PIECES = 4


def along(value, axis, target):
    count = lax.axis_size(axis)
    pairs = [(source, target(source) % count) for source in range(count)]
    return lax.ppermute(value, axis, pairs)


def inverse_norm(values):
    return lax.rsqrt(jnp.sum(values * values, axis=-1, keepdims=True) + eps_norm)


def unit_half(raw):
    values = raw.astype(jnp.float32)
    return (values * inverse_norm(values)).astype(jnp.bfloat16)


def weigh(own, other, scale_ref):
    scores = lax.dot_general(
        own, other, (((1,), (1,)), ((), ())), preferred_element_type=jnp.float32
    )
    return jax.nn.sigmoid(scale_ref[0:1, 0:1] * scores + scale_ref[1:2, 0:1])


def visit(own, other, scale_ref):
    weights = scale_ref[0:1, 0:1] * weigh(own, other, scale_ref)
    return jnp.dot(weights.astype(jnp.bfloat16), other, preferred_element_type=jnp.float32)


def odd_row():
    return lax.axis_index("row") & 1


def unit_back(raw, direction):
    values = raw.astype(jnp.float32)
    inverse = inverse_norm(values)
    unit = values * inverse
    share = jnp.sum(unit * direction, axis=-1, keepdims=True)
    return inverse * (direction - unit * share)


def pieces(rows):
    if rows % (16 * PIECES):
        return [(0, rows)]
    return [(n * rows // PIECES, rows // PIECES) for n in range(PIECES)]


def call(kernel, out_shape, in_specs, out_specs, **more):
    return pl.pallas_call(
        kernel,
        out_shape=out_shape,
        in_specs=in_specs,
        out_specs=out_specs,
        compiler_params=pltpu.CompilerParams(vmem_limit_bytes=LIMIT),
        cost_estimate=pl.CostEstimate(flops=1000, bytes_accessed=1000, transcendentals=0),
        **more,
    )


def pick_kernel(img_ref, txt_ref, out_ref, sems):
    def copy(source):
        parts = [pl.ds(start, size) for start, size in pieces(out_ref.shape[0])]
        copies = [
            pltpu.make_async_copy(source.at[at], out_ref.at[at], sems.at[n])
            for n, at in enumerate(parts)
        ]
        for one in copies:
            one.start()
        for one in copies:
            one.wait()

    odd = odd_row()

    @pl.when(odd == 1)
    def _():
        copy(txt_ref)

    @pl.when(odd != 1)
    def _():
        copy(img_ref)


def pick(img, txt):
    return call(
        pick_kernel,
        jax.ShapeDtypeStruct(img.shape, img.dtype),
        [HBM, HBM],
        VMEM,
        scratch_shapes=[pltpu.SemaphoreType.DMA((len(pieces(img.shape[0])),))],
        name="pick",
    )(img, txt)


def norm_kernel(exponent_ref, offset_ref, img_ref, txt_ref, scale_ref, raw_ref, half_ref, near_ref, sems):
    parts = pieces(img_ref.shape[0])
    copies = []
    for side, source in ((0, img_ref), (1, txt_ref)):
        for n, (start, size) in enumerate(parts):
            at = pl.ds(start, size)
            copies.append(
                pltpu.make_async_copy(source.at[at], raw_ref.at[side, at], sems.at[side, n])
            )
    for copy in copies:
        copy.start()
    scale_ref[0:1] = jnp.exp(jnp.full((1, 128), exponent_ref[0], jnp.float32))
    scale_ref[1:2] = jnp.full((1, 128), offset_ref[0], jnp.float32)
    for side in (0, 1):
        for n, (start, size) in enumerate(parts):
            copies[side * len(parts) + n].wait()
            at = pl.ds(start, size)
            half_ref[side, at] = unit_half(raw_ref[side, at])
    near_ref[...] = half_ref[1 - odd_row()]


def norm(exponent, offset, img, txt):
    rows, width = img.shape
    both = jax.ShapeDtypeStruct((2, rows, width), jnp.bfloat16)
    return call(
        norm_kernel,
        (
            jax.ShapeDtypeStruct((8, 128), jnp.float32),
            both,
            both,
            jax.ShapeDtypeStruct((rows, width), jnp.bfloat16),
        ),
        [SMEM, SMEM, HBM, HBM],
        (VMEM,) * 4,
        scratch_shapes=[pltpu.SemaphoreType.DMA((2, len(pieces(rows))))],
        name="norm",
    )(exponent, offset, img, txt)


def own_kernel(scale_ref, half_ref, dir_ref):
    img, txt = half_ref[0], half_ref[1]
    rows = img.shape[0]
    row = lax.broadcasted_iota(jnp.int32, (rows, rows), 0)
    column = lax.broadcasted_iota(jnp.int32, (rows, rows), 1)
    match = jnp.where(row == column, 1.0, 0.0)
    for side, (own, other) in enumerate(((img, txt), (txt, img))):
        weights = scale_ref[0:1, 0:1] * (weigh(own, other, scale_ref) - match)
        dir_ref[side] = jnp.dot(
            weights.astype(jnp.bfloat16), other, preferred_element_type=jnp.float32
        )


def own_visit(scale, half):
    return call(
        own_kernel,
        jax.ShapeDtypeStruct(half.shape, jnp.float32),
        [VMEM, VMEM],
        VMEM,
        name="own",
    )(scale, half)


def gather_side(side, kinds, blocks, others_ref):
    rows, count = blocks[0].shape[0], 0
    for (at, raw), block in zip(kinds, blocks):
        if at == side:
            held = pl.ds(count * rows, rows)
            others_ref[held] = unit_half(block[...]) if raw else block[...]
            count += 1
    return others_ref[pl.ds(0, count * rows)] if count else None


def visit_all(kinds, blocks, scale_ref, half_ref, dir_ref, acc_ref, others_ref, sides=(0, 1)):
    for side in sides:
        others = gather_side(side, kinds, blocks, others_ref) if blocks else None
        if others is None:
            acc_ref[side] = dir_ref[side]
        else:
            acc_ref[side] = dir_ref[side] + visit(half_ref[side], others, scale_ref)
    for (side, raw), block in zip(kinds, blocks):
        if side >= 2:
            at = odd_row() if side == 2 else 1 - odd_row()
            other = unit_half(block[...]) if raw else block[...]
            acc_ref[at] += visit(half_ref[at], other, scale_ref)


def finish(raw_ref, acc_ref, grad_ref, held_ref, sems):
    copies = []
    for n, (start, size) in enumerate(pieces(held_ref.shape[0])):
        at = pl.ds(start, size)
        held_ref[at] = unit_back(raw_ref[at], acc_ref[at])
        copies.append(pltpu.make_async_copy(held_ref.at[at], grad_ref.at[at], sems.at[n]))
        copies[-1].start()
    for copy in copies:
        copy.wait()


def more_kernel(kinds, scale_ref, half_ref, dir_ref, *rest):
    blocks, (out_ref, others_ref) = rest[:-2], rest[-2:]
    visit_all(kinds, blocks, scale_ref, half_ref, dir_ref, out_ref, others_ref)


def image_kernel(kinds, scale_ref, half_ref, dir_ref, raw_ref, *rest):
    blocks, (out_ref, grad_ref, others_ref, held_ref, sems) = rest[:-5], rest[-5:]
    visit_all(kinds, blocks, scale_ref, half_ref, dir_ref, out_ref, others_ref)
    finish(raw_ref.at[0], out_ref.at[0], grad_ref, held_ref, sems)


def text_kernel(kinds, scale_ref, half_ref, dir_ref, raw_ref, *rest):
    blocks, (grad_ref, acc_ref, others_ref, held_ref, sems) = rest[:-5], rest[-5:]
    visit_all(kinds, blocks, scale_ref, half_ref, dir_ref, acc_ref, others_ref, sides=(1,))
    finish(raw_ref.at[1], acc_ref.at[1], grad_ref, held_ref, sems)


def visits(kernel, scale, half, direction, entries, raw=None):
    kinds, blocks = zip(*entries) if entries else ((), ())
    rows, width = half.shape[1:]
    same = jax.ShapeDtypeStruct(direction.shape, direction.dtype)
    grad = jax.ShapeDtypeStruct((rows, width), jnp.float32)
    operands = [scale, half, direction] + ([] if raw is None else [raw])
    most = max([1] + [sum(kind[0] == side for kind in kinds) for side in (0, 1)])
    scratch = [
        pltpu.VMEM((most * rows, width), jnp.bfloat16),
        pltpu.VMEM(grad.shape, grad.dtype),
        pltpu.SemaphoreType.DMA((len(pieces(rows)),)),
    ]
    if kernel is more_kernel:
        out_shape, out_specs, scratch, aliases = same, VMEM, scratch[:1], {2: 0}
    elif kernel is image_kernel:
        out_shape, out_specs, aliases = (same, grad), (VMEM, HBM), {2: 0}
    else:
        out_shape, out_specs, aliases = grad, HBM, {}
        scratch = [pltpu.VMEM(same.shape, same.dtype)] + scratch
    return call(
        functools.partial(kernel, kinds),
        out_shape,
        [VMEM] * (len(operands) + len(blocks)),
        out_specs,
        input_output_aliases=aliases,
        scratch_shapes=scratch,
        name=kernel.__name__,
    )(*operands, *blocks)


def tied(entries, *others):
    blocks, others = lax.optimization_barrier(([block for _, block in entries], others))
    return [(kind, block) for (kind, _), block in zip(entries, blocks)], *others


def on_device(
    picture_encoder_output, caption_encoder_output, softness_factor_exponent, logit_offset_term
):
    img, txt = picture_encoder_output, caption_encoder_output
    row_extent = min(8, lax.axis_size("row") // 2)
    column_extent = min(4, lax.axis_size("col") // 2)
    paired = row_extent % 2 == 0 and lax.axis_size("row") % 2 == 0
    swap = lambda s: s ^ 1
    held = [pltpu.with_memory_space_constraint(a, pltpu.HBM) for a in (img, txt)]
    text_cols, image_cols, text_rows, image_rows, swapped, last = [], [], [], [], [], []
    for k in range(1, column_extent):
        text_cols.append(((0, True), along(txt, "col", lambda s: s + k)))
    text_cols, col_img = tied(text_cols, img)
    for k in range(1, column_extent):
        image_cols.append(((1, True), along(col_img, "col", lambda s: s - k)))
    scale, raw, half, near = norm(
        softness_factor_exponent.reshape(1), logit_offset_term.reshape(1), *held
    )
    direction = own_visit(scale, half)
    if paired:
        reach = row_extent - 1
        far, row_img = lax.optimization_barrier((pick(*held), img))
        far = along(far, "row", lambda s: s + reach if s % 2 else s - reach)
        far = [((2, True), far)]
        for d in range(2, row_extent, 2):
            text_rows.append(((0, True), along(txt, "row", lambda s: s + d)))
            image_rows.append(((1, True), along(row_img, "row", lambda s: s - d)))
        for entries in (text_cols, text_rows):
            if entries:
                direction = visits(more_kernel, scale, half, direction, entries)
        tied_rows, near, direction = tied(text_rows, near, direction)
        swapped.append(((3, False), along(near, "row", swap)))
        for kind, block in tied_rows:
            swapped.append((kind, along(block, "row", swap)))
        for kind, block in tied(image_rows + far)[0][: len(image_rows)]:
            last.append((kind, along(block, "row", swap)))
        middle = image_cols + image_rows + swapped
        direction = visits(more_kernel, scale, half, direction, middle)
    else:
        far = text_cols + image_cols
        for k in range(1, row_extent):
            far.append(((0, True), along(txt, "row", lambda s: s + k)))
            far.append(((1, True), along(img, "row", lambda s: s - k)))

    direction, image_grad = visits(image_kernel, scale, half, direction, far, raw)
    return image_grad, visits(text_kernel, scale, half, direction, last, raw)


def solution(mesh):
    return jax.shard_map(
        on_device,
        mesh=mesh,
        in_specs=(P(("row", "col"), None), P(("row", "col"), None), P(), P()),
        out_specs=(P(("row", "col"), None), P(("row", "col"), None)),
        check_vma=False,
    )
```

time: 37.2 us -> 38.5 us (1.035)
  the two profiles are of different devices: /device:TPU:19 before, /device:TPU:0 now
where the time goes in v1:
time: 38.5 us; the launch traced here: 38.3 us
  waiting for transfers between devices  14.6 us (38%)
  Pallas kernels  12.9 us (34%)
  starting transfers between devices  8.81 us (23%)
  between operations  2 us (5%)
    ppermute x8, waiting for transfers between devices, along(): return lax.ppermute(value, axis, pairs)  14.6 us
    ppermute x8, starting transfers between devices, along(): return lax.ppermute(value, axis, pairs)  8.81 us
    pallas_call x5, Pallas kernels, visits(): call(functools.partial(kernel, kinds), out_shape, [VMEM] * (len(operands)...  8.57 us
    pallas_call x1, Pallas kernels, norm(): call(norm_kernel, (jax.ShapeDtypeStruct((8, 128), jnp.float32), both, bot...  1.91 us
    pallas_call x1, Pallas kernels, own_visit(): call(own_kernel, jax.ShapeDtypeStruct(half.shape, jnp.float32), [VMEM, VM...  1.33 us
    pallas_call x1, Pallas kernels, pick(): call(pick_kernel, jax.ShapeDtypeStruct(img.shape, img.dtype), [HBM, HBM],...  1.09 us
  transfers between devices with their start and end apart: 8, of which 4 were waited for; matrix products, arithmetic and copies ran while one was open for 0% of the time, Pallas kernels for 29%

profile of v1, /device:TPU:0, one launch (start us, length us, event | category | flops | bytes accessed | tf_op | source)
XLA Modules:
  0.0 38.3 jit_solution(3567324376545956591)
XLA Ops:
  0.6 3.1 %collective-permute-start.1 = (bf16[192,1152]{1,0:T(8,128)(2,1)}, bf16[192,1152]{1,0:T(8,128)(2,1)S(1)}, u32[]{:S(2)}, u32[]{:S(2)}) collective-permute-start(bf16[192,1152]{1,0:T(8,128)(2,1)} %txt_ref.3), channel_id=1, source_target_pairs={{0,1},{1,2},{2,3},{3,0},{4,5},{5,6},{6,7},{7,4},{8,9},{9,10},{10,1... | collective-permute-start | bytes 1327112 | tf_op jit(solution)/shard_map/ppermute | solution.py:21
  3.7 1.5 %collective-permute-start = (bf16[192,1152]{1,0:T(8,128)(2,1)}, bf16[192,1152]{1,0:T(8,128)(2,1)S(1)}, u32[]{:S(2)}, u32[]{:S(2)}) collective-permute-start(bf16[192,1152]{1,0:T(8,128)(2,1)} %txt_ref.3), channel_id=1, source_target_pairs={{0,8},{4,12},{8,16},{12,20},{16,24},{20,28},{24,0},{28,4},{1,9},{5... | collective-permute-start | bytes 1327112 | tf_op jit(solution)/shard_map/ppermute | solution.py:21
  5.2 1.1 %pick.1 = bf16[192,1152]{1,0:T(8,128)(2,1)S(1)} custom-call(bf16[192,1152]{1,0:T(8,128)(2,1)} %img_ref.3, bf16[192,1152]{1,0:T(8,128)(2,1)} %txt_ref.3), custom_call_target="tpu_custom_call" | custom-call | flops 1000 | bytes 1000 | tf_op jit(solution)/shard_map/pick/pallas_call | solution.py:99
  6.3 1.5 %collective-permute-start.3 = (bf16[192,1152]{1,0:T(8,128)(2,1)}, bf16[192,1152]{1,0:T(8,128)(2,1)S(1)}, u32[]{:S(2)}, u32[]{:S(2)}) collective-permute-start(bf16[192,1152]{1,0:T(8,128)(2,1)} %img_ref.3), channel_id=1, source_target_pairs={{0,24},{4,28},{8,0},{12,4},{16,8},{20,12},{24,16},{28,20},{1,25},{... | collective-permute-start | bytes 1327112 | tf_op jit(solution)/shard_map/ppermute | solution.py:21
  7.8 0.1 collective-permute-start.6
  9.2 1.9 %norm.1 = (f32[8,128]{1,0:T(8,128)S(1)}, bf16[2,192,1152]{2,1,0:T(8,128)(2,1)S(1)}, bf16[2,192,1152]{2,1,0:T(8,128)(2,1)S(1)}, bf16[192,1152]{1,0:T(8,128)(2,1)S(1)}) custom-call(f32[1]{0:T(128)} %bitcast.2.exponent_ref, f32[1]{0:T(128)} %bitcast.3.offset_ref, bf16[192,1152]{1,0:T(8,128)(2,1)} %img_ref.3, bf16[192,1152]{1,0:T(8,128)(2,1)} %txt_ref.3), custom_call_target="tpu_custom_call" | custom-call | flops 1000 | bytes 1000 | tf_op jit(solution)/shard_map/norm/pallas_call | solution.py:133
  11.1 1.3 %own.1.dir_ref = f32[2,192,1152]{2,1,0:T(8,128)S(1)} custom-call(f32[8,128]{1,0:T(8,128)S(1)} %get-tuple-element.16.scale_ref, bf16[2,192,1152]{2,1,0:T(8,128)(2,1)S(1)} %get-tuple-element.17.half_ref), custom_call_target="tpu_custom_call" | custom-call | flops 1000 | bytes 1000 | tf_op jit(solution)/shard_map/own/pallas_call | solution.py:162
  12.5 3.7 %collective-permute-done.1.rest_0_ = bf16[192,1152]{1,0:T(8,128)(2,1)S(1)} collective-permute-done((bf16[192,1152]{1,0:T(8,128)(2,1)}, bf16[192,1152]{1,0:T(8,128)(2,1)S(1)}, u32[]{:S(2)}, u32[]{:S(2)}) %collective-permute-start.1) | collective-permute-done | bytes 442400 | tf_op jit(solution)/shard_map/ppermute | solution.py:21
  16.1 1.0 %more_kernel.3.dir_ref = f32[2,192,1152]{2,1,0:T(8,128)S(1)} custom-call(f32[8,128]{1,0:T(8,128)S(1)} %get-tuple-element.16.scale_ref, bf16[2,192,1152]{2,1,0:T(8,128)(2,1)S(1)} %get-tuple-element.17.half_ref, f32[2,192,1152]{2,1,0:T(8,128)S(1)} %own.1.dir_ref, bf16[192,1152]{1,0:T(8,128)(2,1)S(1)} %collective-permute-done.1.rest_0_), custom_call_target="tpu_custom_call", output_to_operand_aliasing={{}: (2, {})} | custom-call | flops 1000 | bytes 1000 | tf_op jit(solution)/shard_map/more_kernel/pallas_call | solution.py:242
  17.1 0.0 copy-start
  17.1 0.9 %collective-permute-done.rest_0_ = bf16[192,1152]{1,0:T(8,128)(2,1)S(1)} collective-permute-done((bf16[192,1152]{1,0:T(8,128)(2,1)}, bf16[192,1152]{1,0:T(8,128)(2,1)S(1)}, u32[]{:S(2)}, u32[]{:S(2)}) %collective-permute-start) | collective-permute-done | bytes 442400 | tf_op jit(solution)/shard_map/ppermute | solution.py:21
  18.0 1.0 %more_kernel.4.dir_ref = f32[2,192,1152]{2,1,0:T(8,128)S(1)} custom-call(f32[8,128]{1,0:T(8,128)S(1)} %get-tuple-element.16.scale_ref, bf16[2,192,1152]{2,1,0:T(8,128)(2,1)S(1)} %get-tuple-element.17.half_ref, f32[2,192,1152]{2,1,0:T(8,128)S(1)} %more_kernel.3.dir_ref, bf16[192,1152]{1,0:T(8,128)(2,1)S(1)} %collective-permute-done.rest_0_), custom_call_target="tpu_custom_call", output_to_operand_aliasing={{}: (2, {})} | custom-call | flops 1000 | bytes 1000 | tf_op jit(solution)/shard_map/more_kernel/pallas_call | solution.py:242
  18.9 0.1 collective-permute-start.4
  19.0 0.5 %collective-permute-start.5 = (bf16[192,1152]{1,0:T(8,128)(2,1)S(1)}, bf16[192,1152]{1,0:T(8,128)(2,1)S(1)}, u32[]{:S(2)}, u32[]{:S(2)}) collective-permute-start(bf16[192,1152]{1,0:T(8,128)(2,1)S(1)} %collective-permute-done.rest_0_), channel_id=1, source_target_pairs={{0,4},{4,0},{8,12},{12,8},{16,20},{20,16},{24,28},{28,24},{1,5},{5... | collective-permute-start | bytes 1327112 | tf_op jit(solution)/shard_map/ppermute | solution.py:21
  19.5 2.1 %collective-permute-start.2 = (bf16[192,1152]{1,0:T(8,128)(2,1)S(1)}, bf16[192,1152]{1,0:T(8,128)(2,1)S(1)}, u32[]{:S(2)}, u32[]{:S(2)}) collective-permute-start(bf16[192,1152]{1,0:T(8,128)(2,1)S(1)} %copy-done), channel_id=1, source_target_pairs={{0,3},{1,0},{2,1},{3,2},{4,7},{5,4},{6,5},{7,6},{8,11},{9,8},{10,9... | collective-permute-start | bytes 1327112 | tf_op jit(solution)/shard_map/ppermute | solution.py:21
  21.6 4.5 %collective-permute-done.3.rest_1_ = bf16[192,1152]{1,0:T(8,128)(2,1)S(1)} collective-permute-done((bf16[192,1152]{1,0:T(8,128)(2,1)}, bf16[192,1152]{1,0:T(8,128)(2,1)S(1)}, u32[]{:S(2)}, u32[]{:S(2)}) %collective-permute-start.3) | collective-permute-done | bytes 442400 | tf_op jit(solution)/shard_map/ppermute | solution.py:21
  26.0 0.0 collective-permute-done.6.rest_0_
  26.0 0.0 collective-permute-start.7
  26.0 0.0 collective-permute-done.4.rest_2_
  26.0 0.0 collective-permute-done.5.rest_3_
  26.0 5.6 %collective-permute-done.2.rest_0_ = bf16[192,1152]{1,0:T(8,128)(2,1)S(1)} collective-permute-done((bf16[192,1152]{1,0:T(8,128)(2,1)S(1)}, bf16[192,1152]{1,0:T(8,128)(2,1)S(1)}, u32[]{:S(2)}, u32[]{:S(2)}) %collective-permute-start.2) | collective-permute-done | bytes 442400 | tf_op jit(solution)/shard_map/ppermute | solution.py:21
  31.7 2.3 %more_kernel.5.dir_ref = f32[2,192,1152]{2,1,0:T(8,128)S(1)} custom-call(f32[8,128]{1,0:T(8,128)S(1)} %get-tuple-element.16.scale_ref, bf16[2,192,1152]{2,1,0:T(8,128)(2,1)S(1)} %get-tuple-element.17.half_ref, f32[2,192,1152]{2,1,0:T(8,128)S(1)} %more_kernel.4.dir_ref, ...), custom_call_target="tpu_custom_call", output_to_operand_aliasing={{}: (2, {})} | custom-call | flops 1000 | bytes 1000 | tf_op jit(solution)/shard_map/more_kernel/pallas_call | solution.py:242
  33.9 2.4 %image_kernel.1 = (f32[2,192,1152]{2,1,0:T(8,128)S(1)}, f32[192,1152]{1,0:T(8,128)}) custom-call(f32[8,128]{1,0:T(8,128)S(1)} %get-tuple-element.16.scale_ref, bf16[2,192,1152]{2,1,0:T(8,128)(2,1)S(1)} %get-tuple-element.17.half_ref, f32[2,192,1152]{2,1,0:T(8,128)S(1)} %more_kernel.5.dir_ref, ...), custom_call_target="tpu_custom_call", output_to_operand_aliasing={{0}: (2, {})} | custom-call | flops 1000 | bytes 1000 | tf_op jit(solution)/shard_map/image_kernel/pallas_call | solution.py:242
  36.4 1.9 %text_kernel.1 = f32[192,1152]{1,0:T(8,128)} custom-call(f32[8,128]{1,0:T(8,128)S(1)} %get-tuple-element.16.scale_ref, bf16[2,192,1152]{2,1,0:T(8,128)(2,1)S(1)} %get-tuple-element.17.half_ref, f32[2,192,1152]{2,1,0:T(8,128)S(1)} %get-tuple-element.28.dir_ref, bf16[2,192,1152]{2,1,0:T(8,128)(2,1)S(1)} %get-tuple-element.25.raw_ref, ...), custom_call_target="tpu_custom_call" | custom-call | flops 1000 | bytes 1000 | tf_op jit(solution)/shard_map/text_kernel/pallas_call | solution.py:242
  (2 shorter events, 0.0 us)
Async XLA Ops:
  0.6 15.5 %collective-permute-start.1 = (bf16[192,1152]{1,0:T(8,128)(2,1)}, bf16[192,1152]{1,0:T(8,128)(2,1)S(1)}, u32[]{:S(2)}, u32[]{:S(2)}) collective-permute-start(bf16[192,1152]{1,0:T(8,128)(2,1)} %txt_ref.3), channel_id=1, source_target_pairs={{0,1},{1,2},{2,3},{3,0},{4,5},{5,6},{6,7},{7,4},{8,9},{9,10},{10,1... | collective-permute-start | bytes 1327112 | tf_op jit(solution)/shard_map/ppermute | solution.py:21
  3.7 14.2 %collective-permute-start = (bf16[192,1152]{1,0:T(8,128)(2,1)}, bf16[192,1152]{1,0:T(8,128)(2,1)S(1)}, u32[]{:S(2)}, u32[]{:S(2)}) collective-permute-start(bf16[192,1152]{1,0:T(8,128)(2,1)} %txt_ref.3), channel_id=1, source_target_pairs={{0,8},{4,12},{8,16},{12,20},{16,24},{20,28},{24,0},{28,4},{1,9},{5... | collective-permute-start | bytes 1327112 | tf_op jit(solution)/shard_map/ppermute | solution.py:21
  6.3 19.7 %collective-permute-start.3 = (bf16[192,1152]{1,0:T(8,128)(2,1)}, bf16[192,1152]{1,0:T(8,128)(2,1)S(1)}, u32[]{:S(2)}, u32[]{:S(2)}) collective-permute-start(bf16[192,1152]{1,0:T(8,128)(2,1)} %img_ref.3), channel_id=1, source_target_pairs={{0,24},{4,28},{8,0},{12,4},{16,8},{20,12},{24,16},{28,20},{1,25},{... | collective-permute-start | bytes 1327112 | tf_op jit(solution)/shard_map/ppermute | solution.py:21
  7.8 18.2 %collective-permute-start.6 = (bf16[192,1152]{1,0:T(8,128)(2,1)S(1)}, bf16[192,1152]{1,0:T(8,128)(2,1)S(1)}, u32[]{:S(2)}, u32[]{:S(2)}) collective-permute-start(bf16[192,1152]{1,0:T(8,128)(2,1)S(1)} %pick.1), channel_id=1, source_target_pairs={{0,20},{4,16},{8,28},{12,24},{16,4},{20,0},{24,12},{28,8},{1,21},{... | collective-permute-start | bytes 1327112 | tf_op jit(solution)/shard_map/ppermute | solution.py:21
  17.1 2.4 %copy-start = (bf16[192,1152]{1,0:T(8,128)(2,1)S(1)}, bf16[192,1152]{1,0:T(8,128)(2,1)}, u32[]{:S(2)}) copy-start(bf16[192,1152]{1,0:T(8,128)(2,1)} %img_ref.3) | copy-start | bytes 1327108
  18.9 7.1 %collective-permute-start.4 = (bf16[192,1152]{1,0:T(8,128)(2,1)S(1)}, bf16[192,1152]{1,0:T(8,128)(2,1)S(1)}, u32[]{:S(2)}, u32[]{:S(2)}) collective-permute-start(bf16[192,1152]{1,0:T(8,128)(2,1)S(1)} %get-tuple-element.23), channel_id=1, source_target_pairs={{0,4},{4,0},{8,12},{12,8},{16,20},{20,16},{24,28},{28,24},{1,5},{5... | collective-permute-start | bytes 1327112 | tf_op jit(solution)/shard_map/ppermute | solution.py:21
  19.0 7.0 %collective-permute-start.5 = (bf16[192,1152]{1,0:T(8,128)(2,1)S(1)}, bf16[192,1152]{1,0:T(8,128)(2,1)S(1)}, u32[]{:S(2)}, u32[]{:S(2)}) collective-permute-start(bf16[192,1152]{1,0:T(8,128)(2,1)S(1)} %collective-permute-done.rest_0_), channel_id=1, source_target_pairs={{0,4},{4,0},{8,12},{12,8},{16,20},{20,16},{24,28},{28,24},{1,5},{5... | collective-permute-start | bytes 1327112 | tf_op jit(solution)/shard_map/ppermute | solution.py:21
  19.5 12.2 %collective-permute-start.2 = (bf16[192,1152]{1,0:T(8,128)(2,1)S(1)}, bf16[192,1152]{1,0:T(8,128)(2,1)S(1)}, u32[]{:S(2)}, u32[]{:S(2)}) collective-permute-start(bf16[192,1152]{1,0:T(8,128)(2,1)S(1)} %copy-done), channel_id=1, source_target_pairs={{0,3},{1,0},{2,1},{3,2},{4,7},{5,4},{6,5},{7,6},{8,11},{9,8},{10,9... | collective-permute-start | bytes 1327112 | tf_op jit(solution)/shard_map/ppermute | solution.py:21
  26.0 10.3 %collective-permute-start.7 = (bf16[192,1152]{1,0:T(8,128)(2,1)S(1)}, bf16[192,1152]{1,0:T(8,128)(2,1)S(1)}, u32[]{:S(2)}, u32[]{:S(2)}) collective-permute-start(bf16[192,1152]{1,0:T(8,128)(2,1)S(1)} %collective-permute-done.3.rest_1_), channel_id=1, source_target_pairs={{0,4},{4,0},{8,12},{12,8},{16,20},{20,16},{24,28},{28,24},{1,5},{5... | collective-permute-start | bytes 1327112 | tf_op jit(solution)/shard_map/ppermute | solution.py:21

commit v2 on v1

v2 whole, which is shorter than its diff:
```python
import functools

import jax
import jax.numpy as jnp
from jax import lax
from jax.experimental import pallas as pl
from jax.experimental.pallas import tpu as pltpu
from jax.sharding import PartitionSpec as P

eps_norm = 1e-06
VMEM = pl.BlockSpec(memory_space=pltpu.VMEM)
SMEM = pl.BlockSpec(memory_space=pltpu.SMEM)
HBM = pl.BlockSpec(memory_space=pltpu.HBM)
LIMIT = 24 * 2**20
PIECES = 4


def along(value, axis, target):
    count = lax.axis_size(axis)
    pairs = [(source, target(source) % count) for source in range(count)]
    return lax.ppermute(value, axis, pairs)


def inverse_norm(values):
    return lax.rsqrt(jnp.sum(values * values, axis=-1, keepdims=True) + eps_norm)


def unit_half(raw):
    values = raw.astype(jnp.float32)
    return (values * inverse_norm(values)).astype(jnp.bfloat16)


def weigh(own, other, scale_ref):
    scores = lax.dot_general(
        own, other, (((1,), (1,)), ((), ())), preferred_element_type=jnp.float32
    )
    return jax.nn.sigmoid(scale_ref[0:1, 0:1] * scores + scale_ref[1:2, 0:1])


def visit(own, other, scale_ref):
    weights = scale_ref[0:1, 0:1] * weigh(own, other, scale_ref)
    return jnp.dot(weights.astype(jnp.bfloat16), other, preferred_element_type=jnp.float32)


def odd_row():
    return lax.axis_index("row") & 1


def unit_back(raw, direction):
    values = raw.astype(jnp.float32)
    inverse = inverse_norm(values)
    unit = values * inverse
    share = jnp.sum(unit * direction, axis=-1, keepdims=True)
    return inverse * (direction - unit * share)


def pieces(rows):
    if rows % (16 * PIECES):
        return [(0, rows)]
    return [(n * rows // PIECES, rows // PIECES) for n in range(PIECES)]


def call(kernel, out_shape, in_specs, out_specs, **more):
    return pl.pallas_call(
        kernel,
        out_shape=out_shape,
        in_specs=in_specs,
        out_specs=out_specs,
        compiler_params=pltpu.CompilerParams(vmem_limit_bytes=LIMIT),
        cost_estimate=pl.CostEstimate(flops=1000, bytes_accessed=1000, transcendentals=0),
        **more,
    )


def pick_kernel(img_ref, txt_ref, out_ref, sems):
    def copy(source):
        parts = [pl.ds(start, size) for start, size in pieces(out_ref.shape[0])]
        copies = [
            pltpu.make_async_copy(source.at[at], out_ref.at[at], sems.at[n])
            for n, at in enumerate(parts)
        ]
        for one in copies:
            one.start()
        for one in copies:
            one.wait()

    odd = odd_row()

    @pl.when(odd == 1)
    def _():
        copy(txt_ref)

    @pl.when(odd != 1)
    def _():
        copy(img_ref)


def pick(img, txt):
    return call(
        pick_kernel,
        jax.ShapeDtypeStruct(img.shape, img.dtype),
        [HBM, HBM],
        VMEM,
        scratch_shapes=[pltpu.SemaphoreType.DMA((len(pieces(img.shape[0])),))],
        name="pick",
    )(img, txt)


def norm_kernel(
    exponent_ref, offset_ref, img_ref, txt_ref, scale_ref, raw_ref, half_ref, img_half, near_ref, sems
):
    parts = pieces(img_ref.shape[0])
    copies = []
    for side, source in ((0, img_ref), (1, txt_ref)):
        for n, (start, size) in enumerate(parts):
            at = pl.ds(start, size)
            copies.append(
                pltpu.make_async_copy(source.at[at], raw_ref.at[side, at], sems.at[side, n])
            )
    for copy in copies:
        copy.start()
    scale_ref[0:1] = jnp.exp(jnp.full((1, 128), exponent_ref[0], jnp.float32))
    scale_ref[1:2] = jnp.full((1, 128), offset_ref[0], jnp.float32)
    for side in (0, 1):
        for n, (start, size) in enumerate(parts):
            copies[side * len(parts) + n].wait()
            at = pl.ds(start, size)
            half_ref[side, at] = unit_half(raw_ref[side, at])
            if side == 0:
                img_half[at] = half_ref[side, at]
    near_ref[...] = half_ref[1 - odd_row()]


def norm(exponent, offset, img, txt):
    rows, width = img.shape
    one = jax.ShapeDtypeStruct((rows, width), jnp.bfloat16)
    both = jax.ShapeDtypeStruct((2, rows, width), jnp.bfloat16)
    return call(
        norm_kernel,
        (
            jax.ShapeDtypeStruct((8, 128), jnp.float32),
            both,
            both,
            one,
            one,
        ),
        [SMEM, SMEM, HBM, HBM],
        (VMEM,) * 5,
        scratch_shapes=[pltpu.SemaphoreType.DMA((2, len(pieces(rows))))],
        name="norm",
    )(exponent, offset, img, txt)


def own_kernel(scale_ref, half_ref, dir_ref):
    img, txt = half_ref[0], half_ref[1]
    rows = img.shape[0]
    row = lax.broadcasted_iota(jnp.int32, (rows, rows), 0)
    column = lax.broadcasted_iota(jnp.int32, (rows, rows), 1)
    match = jnp.where(row == column, 1.0, 0.0)
    for side, (own, other) in enumerate(((img, txt), (txt, img))):
        weights = scale_ref[0:1, 0:1] * (weigh(own, other, scale_ref) - match)
        dir_ref[side] = jnp.dot(
            weights.astype(jnp.bfloat16), other, preferred_element_type=jnp.float32
        )


def own_visit(scale, half):
    return call(
        own_kernel,
        jax.ShapeDtypeStruct(half.shape, jnp.float32),
        [VMEM, VMEM],
        VMEM,
        name="own",
    )(scale, half)


def visit_all(kinds, blocks, scale_ref, half_ref, dir_ref, acc_ref, others_ref):
    rows = half_ref.shape[1]
    held = [others_ref.at[pl.ds(n * rows, rows)] for n in range(len(kinds))]
    order = sorted(range(len(kinds)), key=lambda n: kinds[n][0])
    for place, n in enumerate(order):
        block = blocks[n][...]
        held[place][...] = unit_half(block) if kinds[n][1] else block
    first = 0
    for side in (0, 1):
        count = sum(kind[0] == side for kind in kinds)
        if count:
            others = others_ref[pl.ds(first * rows, count * rows)]
            acc_ref[side] = dir_ref[side] + visit(half_ref[side], others, scale_ref)
        else:
            acc_ref[side] = dir_ref[side]
        first += count
    for place in range(first, len(kinds)):
        at = odd_row() if kinds[order[place]][0] == 2 else 1 - odd_row()
        acc_ref[at] += visit(half_ref[at], held[place][...], scale_ref)


def more_kernel(kinds, scale_ref, half_ref, dir_ref, *rest):
    blocks, (out_ref, others_ref) = rest[: len(kinds)], rest[len(kinds) :]
    visit_all(kinds, blocks, scale_ref, half_ref, dir_ref, out_ref, others_ref)


def finish(raw_ref, acc_ref, grad_ref, held_ref, sems):
    copies = []
    for n, (start, size) in enumerate(pieces(held_ref.shape[0])):
        at = pl.ds(start, size)
        held_ref[at] = unit_back(raw_ref[at], acc_ref[at])
        copies.append(pltpu.make_async_copy(held_ref.at[at], grad_ref.at[at], sems.at[n]))
        copies[-1].start()
    return copies


def last_kernel(kinds, scale_ref, half_ref, dir_ref, raw_ref, *rest):
    blocks, (img_grad, txt_grad, acc_ref, others_ref, held_ref, sems) = (
        rest[: len(kinds)],
        rest[len(kinds) :],
    )
    visit_all(kinds, blocks, scale_ref, half_ref, dir_ref, acc_ref, others_ref)
    copies = []
    for side, grad_ref in ((0, img_grad), (1, txt_grad)):
        copies += finish(
            raw_ref.at[side], acc_ref.at[side], grad_ref, held_ref.at[side], sems.at[side]
        )
    for copy in copies:
        copy.wait()


def more_visits(scale, half, direction, entries, give=True):
    kinds, blocks = zip(*entries)
    rows, width = half.shape[1:]
    sums = jax.ShapeDtypeStruct(direction.shape, direction.dtype)
    halves = (len(kinds) * rows, width)
    return call(
        functools.partial(more_kernel, kinds),
        (sums, jax.ShapeDtypeStruct(halves, jnp.bfloat16)) if give else sums,
        [VMEM] * (3 + len(blocks)),
        (VMEM, VMEM) if give else VMEM,
        scratch_shapes=[] if give else [pltpu.VMEM(halves, jnp.bfloat16)],
        input_output_aliases={2: 0},
        name="more",
    )(scale, half, direction, *blocks)


def last_visits(scale, half, direction, raw, entries):
    kinds, blocks = zip(*entries) if entries else ((), ())
    rows, width = half.shape[1:]
    grad = jax.ShapeDtypeStruct((rows, width), jnp.float32)
    return call(
        functools.partial(last_kernel, kinds),
        (grad, grad),
        [VMEM] * (4 + len(blocks)),
        (HBM, HBM),
        scratch_shapes=[
            pltpu.VMEM(direction.shape, direction.dtype),
            pltpu.VMEM((max(1, len(kinds)) * rows, width), jnp.bfloat16),
            pltpu.VMEM(direction.shape, direction.dtype),
            pltpu.SemaphoreType.DMA((2, len(pieces(rows)))),
        ],
        name="last",
    )(scale, half, direction, raw, *blocks)


def tied(entries, *others):
    blocks, others = lax.optimization_barrier(([block for _, block in entries], others))
    return [(kind, block) for (kind, _), block in zip(entries, blocks)], *others


def on_device(
    picture_encoder_output, caption_encoder_output, softness_factor_exponent, logit_offset_term
):
    img, txt = picture_encoder_output, caption_encoder_output
    row_extent = min(8, lax.axis_size("row") // 2)
    column_extent = min(4, lax.axis_size("col") // 2)
    paired = row_extent % 2 == 0 and lax.axis_size("row") % 2 == 0
    swap = lambda s: s ^ 1
    held = [pltpu.with_memory_space_constraint(a, pltpu.HBM) for a in (img, txt)]
    text_cols, image_cols, text_rows, image_rows, swapped, last = [], [], [], [], [], []
    for k in range(1, column_extent):
        text_cols.append(((0, True), along(txt, "col", lambda s: s + k)))
    scale, raw, half, img_half, near = norm(
        softness_factor_exponent.reshape(1), logit_offset_term.reshape(1), *held
    )
    for k in range(1, column_extent):
        image_cols.append(((1, False), along(img_half, "col", lambda s: s - k)))
    direction = own_visit(scale, half)
    if not paired:
        for k in range(1, row_extent):
            text_rows.append(((0, True), along(txt, "row", lambda s: s + k)))
            image_rows.append(((1, False), along(img_half, "row", lambda s: s - k)))
        last = text_cols + image_cols + text_rows + image_rows
        return last_visits(scale, half, direction, raw, last)

    reach = row_extent - 1
    far = along(pick(*held), "row", lambda s: s + reach if s % 2 else s - reach)
    for d in range(2, row_extent, 2):
        text_rows.append(((0, True), along(txt, "row", lambda s: s + d)))
        image_rows.append(((1, False), along(img_half, "row", lambda s: s - d)))
    if text_cols:
        direction = more_visits(scale, half, direction, text_cols, False)
    if text_rows:
        direction, halves = more_visits(scale, half, direction, text_rows)
        for n in range(len(text_rows)):
            block = halves[n * img.shape[0] : (n + 1) * img.shape[0]]
            last.append(((0, False), along(block, "row", swap)))
    near, far, direction = lax.optimization_barrier((near, far, direction))
    last.append(((3, False), along(near, "row", swap)))
    for kind, block in image_rows:
        last.append((kind, along(block, "row", swap)))
    if image_rows:
        direction = more_visits(scale, half, direction, image_rows, False)
    direction = more_visits(scale, half, direction, [((2, True), far)] + image_cols, False)
    return last_visits(scale, half, direction, raw, last)


def solution(mesh):
    return jax.shard_map(
        on_device,
        mesh=mesh,
        in_specs=(P(("row", "col"), None), P(("row", "col"), None), P(), P()),
        out_specs=(P(("row", "col"), None), P(("row", "col"), None)),
        check_vma=False,
    )
```

time: 38.5 us -> 33.7 us (0.88)
  the two profiles are of different devices: /device:TPU:0 before, /device:TPU:19 now
where the time goes in v2:
time: 33.7 us; the launch traced here: 33.5 us
  waiting for transfers between devices  12.4 us (37%)
  Pallas kernels  12.2 us (36%)
  starting transfers between devices  6.85 us (20%)
  between operations  2.01 us (6%)
    ppermute x8, waiting for transfers between devices, along(): return lax.ppermute(value, axis, pairs)  12.4 us
    ppermute x8, starting transfers between devices, along(): return lax.ppermute(value, axis, pairs)  6.85 us
    pallas_call x4, Pallas kernels, more_visits(): call(functools.partial(more_kernel, kinds), (sums, jax.ShapeDtypeStruct(h...  4.59 us
    pallas_call x1, Pallas kernels, last_visits(): call(functools.partial(last_kernel, kinds), (grad, grad), [VMEM] * (4 + l...  3.28 us
    pallas_call x1, Pallas kernels, norm(): call(norm_kernel, (jax.ShapeDtypeStruct((8, 128), jnp.float32), both, bot...  1.95 us
    pallas_call x1, Pallas kernels, own_visit(): call(own_kernel, jax.ShapeDtypeStruct(half.shape, jnp.float32), [VMEM, VM...  1.33 us
    pallas_call x1, Pallas kernels, pick(): call(pick_kernel, jax.ShapeDtypeStruct(img.shape, img.dtype), [HBM, HBM],...  1.09 us
  transfers between devices with their start and end apart: 8, of which 2 were waited for; matrix products, arithmetic and copies ran while one was open for 0% of the time, Pallas kernels for 27%

profile of v2, /device:TPU:19, one launch (start us, length us, event | category | flops | bytes accessed | tf_op | source)
XLA Modules:
  0.0 33.5 jit_solution(2017973934446442878)
XLA Ops:
  0.6 1.3 %collective-permute-start.1 = (bf16[192,1152]{1,0:T(8,128)(2,1)}, bf16[192,1152]{1,0:T(8,128)(2,1)S(1)}, u32[]{:S(2)}, u32[]{:S(2)}) collective-permute-start(bf16[192,1152]{1,0:T(8,128)(2,1)} %txt_ref.3), channel_id=1, source_target_pairs={{0,1},{1,2},{2,3},{3,0},{4,5},{5,6},{6,7},{7,4},{8,9},{9,10},{10,1... | collective-permute-start | bytes 1327112 | tf_op jit(solution)/shard_map/ppermute | solution.py:21
  2.0 1.2 %collective-permute-start.2 = (bf16[192,1152]{1,0:T(8,128)(2,1)}, bf16[192,1152]{1,0:T(8,128)(2,1)S(1)}, u32[]{:S(2)}, u32[]{:S(2)}) collective-permute-start(bf16[192,1152]{1,0:T(8,128)(2,1)} %txt_ref.3), channel_id=1, source_target_pairs={{0,8},{4,12},{8,16},{12,20},{16,24},{20,28},{24,0},{28,4},{1,9},{5... | collective-permute-start | bytes 1327112 | tf_op jit(solution)/shard_map/ppermute | solution.py:21
  3.2 1.1 %pick.1 = bf16[192,1152]{1,0:T(8,128)(2,1)S(1)} custom-call(bf16[192,1152]{1,0:T(8,128)(2,1)} %img_ref.3, bf16[192,1152]{1,0:T(8,128)(2,1)} %txt_ref.3), custom_call_target="tpu_custom_call" | custom-call | flops 1000 | bytes 1000 | tf_op jit(solution)/shard_map/pick/pallas_call | solution.py:99
  4.3 1.4 %collective-permute-start = (bf16[192,1152]{1,0:T(8,128)(2,1)S(1)}, bf16[192,1152]{1,0:T(8,128)(2,1)S(1)}, u32[]{:S(2)}, u32[]{:S(2)}) collective-permute-start(bf16[192,1152]{1,0:T(8,128)(2,1)S(1)} %pick.1), channel_id=1, source_target_pairs={{0,20},{4,16},{8,28},{12,24},{16,4},{20,0},{24,12},{28,8},{1,21},{... | collective-permute-start | bytes 1327112 | tf_op jit(solution)/shard_map/ppermute | solution.py:21
  7.0 1.9 %norm.1 = (f32[8,128]{1,0:T(8,128)S(1)}, bf16[2,192,1152]{2,1,0:T(8,128)(2,1)S(1)}, bf16[2,192,1152]{2,1,0:T(8,128)(2,1)S(1)}, bf16[192,1152]{1,0:T(8,128)(2,1)S(1)}, bf16[192,1152]{1,0:T(8,128)(2,1)S(1)}) custom-call(f32[1]{0:T(128)} %bitcast.2.exponent_ref, f32[1]{0:T(128)} %bitcast.3.offset_ref, bf16[192,1152]{1,0:T(8,128)(2,1)} %img_ref.3, ...), custom_call_target="tpu_custom_call" | custom-call | flops 1000 | bytes 1000 | tf_op jit(solution)/shard_map/norm/pallas_call | solution.py:138
  9.0 1.3 %collective-permute-start.3 = (bf16[192,1152]{1,0:T(8,128)(2,1)S(1)}, bf16[192,1152]{1,0:T(8,128)(2,1)S(1)}, u32[]{:S(2)}, u32[]{:S(2)}) collective-permute-start(bf16[192,1152]{1,0:T(8,128)(2,1)S(1)} %get-tuple-element.17), channel_id=1, source_target_pairs={{0,24},{4,28},{8,0},{12,4},{16,8},{20,12},{24,16},{28,20},{1,25},{... | collective-permute-start | bytes 1327112 | tf_op jit(solution)/shard_map/ppermute | solution.py:21
  10.3 0.2 collective-permute-start.4
  10.4 1.3 %own.1.dir_ref = f32[2,192,1152]{2,1,0:T(8,128)S(1)} custom-call(f32[8,128]{1,0:T(8,128)S(1)} %get-tuple-element.12.scale_ref, bf16[2,192,1152]{2,1,0:T(8,128)(2,1)S(1)} %get-tuple-element.13.half_ref), custom_call_target="tpu_custom_call" | custom-call | flops 1000 | bytes 1000 | tf_op jit(solution)/shard_map/own/pallas_call | solution.py:168
  11.8 0.2 collective-permute-done.1.rest_0_
  11.9 1.0 %more.4.dir_ref = f32[2,192,1152]{2,1,0:T(8,128)S(1)} custom-call(f32[8,128]{1,0:T(8,128)S(1)} %get-tuple-element.12.scale_ref, bf16[2,192,1152]{2,1,0:T(8,128)(2,1)S(1)} %get-tuple-element.13.half_ref, f32[2,192,1152]{2,1,0:T(8,128)S(1)} %own.1.dir_ref, bf16[192,1152]{1,0:T(8,128)(2,1)S(1)} %collective-permute-done.1.rest_0_), custom_call_target="tpu_custom_call", output_to_operand_aliasing={{}: (2, {})} | custom-call | flops 1000 | bytes 1000 | tf_op jit(solution)/shard_map/more/pallas_call | solution.py:233
  12.9 0.0 collective-permute-done.2.rest_0_
  12.9 1.0 %more.5 = (f32[2,192,1152]{2,1,0:T(8,128)S(1)}, bf16[192,1152]{1,0:T(8,128)(2,1)S(1)}) custom-call(f32[8,128]{1,0:T(8,128)S(1)} %get-tuple-element.12.scale_ref, bf16[2,192,1152]{2,1,0:T(8,128)(2,1)S(1)} %get-tuple-element.13.half_ref, f32[2,192,1152]{2,1,0:T(8,128)S(1)} %more.4.dir_ref, ...), custom_call_target="tpu_custom_call", output_to_operand_aliasing={{0}: (2, {})} | custom-call | flops 1000 | bytes 1000 | tf_op jit(solution)/shard_map/more/pallas_call | solution.py:233
  13.9 12.2 %collective-permute-done.rest_0_ = bf16[192,1152]{1,0:T(8,128)(2,1)S(1)} collective-permute-done((bf16[192,1152]{1,0:T(8,128)(2,1)S(1)}, bf16[192,1152]{1,0:T(8,128)(2,1)S(1)}, u32[]{:S(2)}, u32[]{:S(2)}) %collective-permute-start) | collective-permute-done | bytes 442400 | tf_op jit(solution)/shard_map/ppermute | solution.py:21
  26.1 0.9 %collective-permute-start.6 = (bf16[192,1152]{1,0:T(8,128)(2,1)S(1)}, bf16[192,1152]{1,0:T(8,128)(2,1)S(1)}, u32[]{:S(2)}, u32[]{:S(2)}) collective-permute-start(bf16[192,1152]{1,0:T(8,128)(2,1)S(1)} %get-tuple-element.21), channel_id=1, source_target_pairs={{0,4},{4,0},{8,12},{12,8},{16,20},{20,16},{24,28},{28,24},{1,5},{5... | collective-permute-start | bytes 1327112 | tf_op jit(solution)/shard_map/ppermute | solution.py:21
  27.0 0.0 collective-permute-start.5
  27.0 0.0 collective-permute-done.3.rest_0_
  27.0 0.5 %collective-permute-start.7 = (bf16[192,1152]{1,0:T(8,128)(2,1)S(1)}, bf16[192,1152]{1,0:T(8,128)(2,1)S(1)}, u32[]{:S(2)}, u32[]{:S(2)}) collective-permute-start(bf16[192,1152]{1,0:T(8,128)(2,1)S(1)} %collective-permute-done.3.rest_0_), channel_id=1, source_target_pairs={{0,4},{4,0},{8,12},{12,8},{16,20},{20,16},{24,28},{28,24},{1,5},{5... | collective-permute-start | bytes 1327112 | tf_op jit(solution)/shard_map/ppermute | solution.py:21
  27.5 0.9 %more.6.dir_ref = f32[2,192,1152]{2,1,0:T(8,128)S(1)} custom-call(f32[8,128]{1,0:T(8,128)S(1)} %get-tuple-element.12.scale_ref, bf16[2,192,1152]{2,1,0:T(8,128)(2,1)S(1)} %get-tuple-element.13.half_ref, f32[2,192,1152]{2,1,0:T(8,128)S(1)} %get-tuple-element.16.dir_ref, ...), custom_call_target="tpu_custom_call", output_to_operand_aliasing={{}: (2, {})} | custom-call | flops 1000 | bytes 1000 | tf_op jit(solution)/shard_map/more/pallas_call | solution.py:233
  28.4 0.0 collective-permute-done.4.rest_1_
  28.4 1.8 %more.7.dir_ref = f32[2,192,1152]{2,1,0:T(8,128)S(1)} custom-call(f32[8,128]{1,0:T(8,128)S(1)} %get-tuple-element.12.scale_ref, bf16[2,192,1152]{2,1,0:T(8,128)(2,1)S(1)} %get-tuple-element.13.half_ref, f32[2,192,1152]{2,1,0:T(8,128)S(1)} %more.6.dir_ref, bf16[192,1152]{1,0:T(8,128)(2,1)S(1)} %collective-permute-done.rest_0_, ...), custom_call_target="tpu_custom_call", output_to_operand_aliasing={{}: (2, {})} | custom-call | flops 1000 | bytes 1000 | tf_op jit(solution)/shard_map/more/pallas_call | solution.py:233
  30.2 0.0 collective-permute-done.6.rest_1_
  30.2 0.0 collective-permute-done.5.rest_0_
  30.2 0.0 collective-permute-done.7.rest_2_
  30.2 3.3 %last.1 = (f32[192,1152]{1,0:T(8,128)}, f32[192,1152]{1,0:T(8,128)}) custom-call(f32[8,128]{1,0:T(8,128)S(1)} %get-tuple-element.12.scale_ref, bf16[2,192,1152]{2,1,0:T(8,128)(2,1)S(1)} %get-tuple-element.13.half_ref, f32[2,192,1152]{2,1,0:T(8,128)S(1)} %more.7.dir_ref, bf16[2,192,1152]{2,1,0:T(8,128)(2,1)S(1)} %get-tuple-element.19.raw_ref, ...), custom_call_target="tpu_custom_call" | custom-call | flops 1000 | bytes 1000 | tf_op jit(solution)/shard_map/last/pallas_call | solution.py:248
Async XLA Ops:
  0.6 11.3 %collective-permute-start.1 = (bf16[192,1152]{1,0:T(8,128)(2,1)}, bf16[192,1152]{1,0:T(8,128)(2,1)S(1)}, u32[]{:S(2)}, u32[]{:S(2)}) collective-permute-start(bf16[192,1152]{1,0:T(8,128)(2,1)} %txt_ref.3), channel_id=1, source_target_pairs={{0,1},{1,2},{2,3},{3,0},{4,5},{5,6},{6,7},{7,4},{8,9},{9,10},{10,1... | collective-permute-start | bytes 1327112 | tf_op jit(solution)/shard_map/ppermute | solution.py:21
  2.0 10.9 %collective-permute-start.2 = (bf16[192,1152]{1,0:T(8,128)(2,1)}, bf16[192,1152]{1,0:T(8,128)(2,1)S(1)}, u32[]{:S(2)}, u32[]{:S(2)}) collective-permute-start(bf16[192,1152]{1,0:T(8,128)(2,1)} %txt_ref.3), channel_id=1, source_target_pairs={{0,8},{4,12},{8,16},{12,20},{16,24},{20,28},{24,0},{28,4},{1,9},{5... | collective-permute-start | bytes 1327112 | tf_op jit(solution)/shard_map/ppermute | solution.py:21
  4.3 21.8 %collective-permute-start = (bf16[192,1152]{1,0:T(8,128)(2,1)S(1)}, bf16[192,1152]{1,0:T(8,128)(2,1)S(1)}, u32[]{:S(2)}, u32[]{:S(2)}) collective-permute-start(bf16[192,1152]{1,0:T(8,128)(2,1)S(1)} %pick.1), channel_id=1, source_target_pairs={{0,20},{4,16},{8,28},{12,24},{16,4},{20,0},{24,12},{28,8},{1,21},{... | collective-permute-start | bytes 1327112 | tf_op jit(solution)/shard_map/ppermute | solution.py:21
  9.0 18.0 %collective-permute-start.3 = (bf16[192,1152]{1,0:T(8,128)(2,1)S(1)}, bf16[192,1152]{1,0:T(8,128)(2,1)S(1)}, u32[]{:S(2)}, u32[]{:S(2)}) collective-permute-start(bf16[192,1152]{1,0:T(8,128)(2,1)S(1)} %get-tuple-element.17), channel_id=1, source_target_pairs={{0,24},{4,28},{8,0},{12,4},{16,8},{20,12},{24,16},{28,20},{1,25},{... | collective-permute-start | bytes 1327112 | tf_op jit(solution)/shard_map/ppermute | solution.py:21
  10.3 18.1 %collective-permute-start.4 = (bf16[192,1152]{1,0:T(8,128)(2,1)S(1)}, bf16[192,1152]{1,0:T(8,128)(2,1)S(1)}, u32[]{:S(2)}, u32[]{:S(2)}) collective-permute-start(bf16[192,1152]{1,0:T(8,128)(2,1)S(1)} %get-tuple-element.17), channel_id=1, source_target_pairs={{0,3},{1,0},{2,1},{3,2},{4,7},{5,4},{6,5},{7,6},{8,11},{9,8},{10,9... | collective-permute-start | bytes 1327112 | tf_op jit(solution)/shard_map/ppermute | solution.py:21
  26.1 4.1 %collective-permute-start.6 = (bf16[192,1152]{1,0:T(8,128)(2,1)S(1)}, bf16[192,1152]{1,0:T(8,128)(2,1)S(1)}, u32[]{:S(2)}, u32[]{:S(2)}) collective-permute-start(bf16[192,1152]{1,0:T(8,128)(2,1)S(1)} %get-tuple-element.21), channel_id=1, source_target_pairs={{0,4},{4,0},{8,12},{12,8},{16,20},{20,16},{24,28},{28,24},{1,5},{5... | collective-permute-start | bytes 1327112 | tf_op jit(solution)/shard_map/ppermute | solution.py:21
  27.0 3.2 %collective-permute-start.5 = (bf16[192,1152]{1,0:T(8,128)(2,1)S(1)}, bf16[192,1152]{1,0:T(8,128)(2,1)S(1)}, u32[]{:S(2)}, u32[]{:S(2)}) collective-permute-start(bf16[192,1152]{1,0:T(8,128)(2,1)S(1)} %get-tuple-element.20), channel_id=1, source_target_pairs={{0,4},{4,0},{8,12},{12,8},{16,20},{20,16},{24,28},{28,24},{1,5},{5... | collective-permute-start | bytes 1327112 | tf_op jit(solution)/shard_map/ppermute | solution.py:21
  27.0 3.2 %collective-permute-start.7 = (bf16[192,1152]{1,0:T(8,128)(2,1)S(1)}, bf16[192,1152]{1,0:T(8,128)(2,1)S(1)}, u32[]{:S(2)}, u32[]{:S(2)}) collective-permute-start(bf16[192,1152]{1,0:T(8,128)(2,1)S(1)} %collective-permute-done.3.rest_0_), channel_id=1, source_target_pairs={{0,4},{4,0},{8,12},{12,8},{16,20},{20,16},{24,28},{28,24},{1,5},{5... | collective-permute-start | bytes 1327112 | tf_op jit(solution)/shard_map/ppermute | solution.py:21
